TPU v7x, 32 devices: a whole 2x2x4 slice. The times are simulated.
32 devices in a mesh: slab: 8 (over z, y), grp: 4 (over x, core).
Axes of the slice: x: 2, y: 2, z: 4, core: 2. Of those that a mesh axis runs over, the one named last changes fastest.
Arguments:
- blocks: bfloat16 [4, 4, 128, 128, 128], P('grp', None, 'slab'), may hold values from -6 to 6
- coords: int32 [4, 8, 4, 2], P('grp', 'slab'), may hold values from 0 to 15
- counts: int32 [4, 8], P('grp', 'slab'), may hold values from 1 to 4, as said below
- omega1: bfloat16 [128, 512], replicated, may hold values from -0.5 to 0.5
- omega2: bfloat16 [2048, 512], replicated, may hold values from -0.5 to 0.5
- omega3: bfloat16 [2048, 512], replicated, may hold values from -0.125 to 0.125
Outputs:
- core_sketch: float32 [512, 512, 512], P(None, 'slab', 'grp')
Inputs may be any that keep to these rules, and one draw needn't show every extreme that they name: counts[g, s] slots are live in the list of group g on slab s; slots from it on are ignored. Some list holds 4 live slots in every draw.
All inputs are finite; a program needn't handle non-finite values.
Results may differ from a plain program's by a relative error of at most 0.0041.
Values may be sent and summed in bfloat16 or wider, within the bound.
A program may use at most 128 MiB of HBM per device.

v0:
```python
import jax
import jax.numpy as jnp
from jax import lax
from jax.sharding import PartitionSpec as P


def contract(running, one_block, coordinate, omega2, third_cols):
    block_edge = one_block.shape[-1]
    third_rows = lax.dynamic_slice_in_dim(third_cols, coordinate[1] * block_edge, block_edge, 0)
    second_rows = lax.dynamic_slice_in_dim(omega2, coordinate[0] * block_edge, block_edge, 0)
    after_third = jnp.einsum(
        "iab,bs->ias", one_block, third_rows, preferred_element_type=jnp.float32
    ).astype(jnp.bfloat16)
    return running + jnp.einsum(
        "ias,ar->sir", after_third, second_rows, preferred_element_type=jnp.float32
    )


def local(blocks, coords, counts, omega1, omega2, omega3):
    own_blocks = blocks[0]
    places = coords[0, 0]
    live_count = counts[0, 0]
    slab_depth = own_blocks.shape[1]
    sketch_width = omega2.shape[1]
    empty_sketch = jnp.zeros((omega3.shape[1], slab_depth, sketch_width), jnp.float32)

    def own_step(position, running):
        return contract(running, own_blocks[position], places[position], omega2, omega3)

    sketch = lax.fori_loop(0, live_count, own_step, empty_sketch)
    reduced = lax.psum_scatter(sketch, "grp", scatter_dimension=0, tiled=True).astype(jnp.bfloat16)
    folded = lax.all_to_all(reduced, "slab", split_axis=2, concat_axis=1, tiled=True)
    return jnp.einsum("ir,sip->rps", omega1, folded, preferred_element_type=jnp.float32)


def solution(mesh):
    in_specs = (
        P("grp", None, "slab", None, None),
        P("grp", "slab", None, None),
        P("grp", "slab"),
        P(),
        P(),
        P(),
    )
    out_specs = P(None, "slab", "grp")
    return jax.shard_map(local, mesh=mesh, in_specs=in_specs, out_specs=out_specs, check_vma=False)
```

profile of v0, /device:TPU:0, one launch (start us, length us, event | category | flops | bytes accessed | tf_op | source)
XLA Modules:
  0.0 320.5 jit_solution(2245688444291989182)
XLA Ops:
  6.5 0.0 copy-start
  6.5 0.0 reduce-scatter.2.cloned.1.call-start
  6.5 0.0 copy-start.1
  6.5 8.3 %broadcast_in_dim.3 = f32[512,16,512]{0,2,1:T(8,128)} broadcast(f32[]{:T(128)} %constant.15.clone.1), dimensions={} | broadcast | bytes 16777220 | tf_op jit(solution)/shard_map/broadcast_in_dim | solution.py:25
  14.9 0.0 copy-done.1
  14.9 18.2 %while.10 = (s32[]{:T(128)}, f32[512,16,512]{0,2,1:T(8,128)}, s32[]{:T(128)}, s32[4,2]{0,1:T(2,128)S(1)}, bf16[2048,512]{1,0:T(8,128)(2,1)}, /*index=5*/bf16[4,1...) while((s32[]{:T(128)}, f32[512,16,512]{0,2,1:T(8,128)}, ...), condition=%wide.region_1.0_spmd, body=%wide.region_0.0_spmd.sunk | while | flops 1347420160 | bytes 34341160 | solution.py:30
  15.5 0.1 constant_dynamic-slice_fusion.2
  15.6 0.5 fusion.27
  17.3 15.1 %bitcast_add_fusion.2 = f32[512,16,512]{0,2,1:T(8,128)} fusion(f32[512,16,512]{0,2,1:T(8,128)} %get-tuple-element.149, bf16[4,16,128,128]{3,2,1,0:T(8,128)(2,1)} %get-tuple-element.165, s32[]{:T(128)S(6)} %select_n.13, bf16[2048,512]{1,0:T(8,128)(2,1)} %get-tuple-element.166, s32[]{:T(128)S(6)} %select_n.14, bf16[2048,512]{1,0:T(8,128)(2,1)} %get-tuple-element.164, ...), kind=kOutput, calls=%fused_computation.clone.1 | convolution fusion | flops 1347420160 | bytes 34340876 | tf_op jit(solution)/shard_map/while/body/ias,ar->sir/dot_general | solution.py:14
  33.1 17.7 %copy.18 = f32[512,16,512]{0,1,2:T(8,128)} copy(f32[512,16,512]{0,2,1:T(8,128)} %get-tuple-element.43) | data formatting | bytes 33554432 | tf_op jit(solution)/shard_map/while | solution.py:30
  50.8 0.0 reduce-scatter.2.cloned.1.call-update
  50.8 181.6 %reduce-scatter.2.cloned.1.call-done = f32[128,16,512]{0,1,2:T(8,128)} async-done(((f32[512,16,512]{0,1,2:T(8,128)}), f32[128,16,512]{0,1,2:T(8,128)}) %reduce-scatter.2.cloned.1.call-update) | async-done | bytes 4194320 | tf_op jit(solution)/shard_map/reduce_scatter | solution.py:31
  232.4 2.5 convert_element_type.6
  234.9 53.6 %all_to_all.18 = bf16[128,16,512]{0,1,2:T(8,128)(2,1)S(1)} all-to-all(bf16[128,16,512]{0,1,2:T(8,128)(2,1)S(1)} %convert_element_type.6), channel_id=1, replica_groups=mesh['slab'=8,'grp'=4] {'slab'}, dimensions={2} | all-to-all | bytes 4194304 | tf_op jit(solution)/shard_map/all_to_all | solution.py:32
  288.4 0.5 copy.20
  289.0 0.0 copy-done
  289.0 8.2 %convolution_bitcast_fusion = f32[512,64,128]{0,2,1:T(8,128)} fusion(bf16[128,128,64]{0,2,1:T(8,128)(2,1)S(1)} %bitcast.40, bf16[128,512]{1,0:T(8,128)(2,1)S(1)} %copy-done), kind=kOutput, calls=%fused_computation.11 | convolution fusion | flops 1073741824 | bytes 19005440 | tf_op jit(solution)/shard_map/ir,sip->rps/dot_general | solution.py:33
  297.2 16.5 %copy.22 = f32[512,64,128]{2,1,0:T(8,128)} copy(f32[512,64,128]{0,2,1:T(8,128)} %convolution_bitcast_fusion) | data formatting | bytes 33554432 | tf_op jit(solution)/shard_map/ir,sip->rps/transpose | solution.py:33
Async XLA Ops:
  6.5 282.5 %copy-start = (bf16[128,512]{1,0:T(8,128)(2,1)S(1)}, bf16[128,512]{1,0:T(8,128)(2,1)}, u32[]{:S(2)}) copy-start(bf16[128,512]{1,0:T(8,128)(2,1)} %param.11) | copy-start | bytes 393220
  6.5 225.9 %reduce-scatter.2.cloned.1.call-start = ((), (), s32[]{:S(2)}) async-start(), calls=%async_computation.2 | async-start | bytes 20971520 | tf_op jit(solution)/shard_map/reduce_scatter | solution.py:31
  6.5 8.3 %copy-start.1 = (s32[1,1,4,2]{2,3,1,0:T(2,128)S(1)}, s32[1,1,4,2]{2,3,1,0:T(2,128)}, u32[]{:S(2)}) copy-start(s32[1,1,4,2]{2,3,1,0:T(2,128)} %param.9) | copy-start | bytes 100
Sparse Core Ops, SparseCore 0:
  50.9 181.4 reduce-scatter.1
where the time goes:
time: 321 us
  waiting for transfers between devices  182 us (57%)
  blocking collectives  53.6 us (17%)
  local copies, waits for them, and re-layouts  43.6 us (14%)
  matrix products  23.3 us (7%)
  between operations  13.4 us (4%)
    reduce_scatter x1, waiting for transfers between devices, local(): lax.psum_scatter(sketch, 'grp', scatter_dimension=0, tiled=True)  182 us
    all_to_all x1, blocking collectives, local(): lax.all_to_all(reduced, 'slab', split_axis=2, concat_axis=1, tiled=True)  53.6 us
    while x1, local copies, waits for them, and re-layouts, local(): sketch = lax.fori_loop(0, live_count, own_step, empty_sketch)  17.7 us
    transpose x1, local copies, waits for them, and re-layouts, local(): jnp.einsum('ir,sip->rps', omega1, folded, preferred_element_type=jnp.floa...  16.5 us
    dot_general x1, matrix products, contract(): jnp.einsum('ias,ar->sir', after_third, second_rows, preferred_element_typ...  15.1 us
    broadcast_in_dim x1, local copies, waits for them, and re-layouts, local(): jnp.zeros((omega3.shape[1], slab_depth, sketch_width), jnp.float32)  8.31 us
    dot_general x1, matrix products, local(): jnp.einsum('ir,sip->rps', omega1, folded, preferred_element_type=jnp.floa...  8.22 us
  transfers between devices with their start and end apart: 1, of which 1 were waited for; matrix products, arithmetic and copies ran while one was open for 0% of the time, Pallas kernels for 0%

commit v1 on v0

v1 whole, which is shorter than its diff:
```python
import functools

import jax
import jax.numpy as jnp
from jax import lax
from jax.experimental import pallas as pl
from jax.experimental.pallas import tpu as pltpu
from jax.sharding import PartitionSpec as P

MESH = pl.DeviceIdType.MESH
LANES = 128


def exchange_kernel(
    n_slab, chunk, blocks, meta, omega2, omega3, out,
    held, metas, places, second, third, second_cat, after_cat, folded,
    load_sem, own_sem, meta_send, meta_recv, block_send, block_recv, fold_send, fold_recv,
):
    slab, grp = lax.axis_index("slab"), lax.axis_index("grp")
    n_slots, depth, edge = held.shape[1], held.shape[2], held.shape[3]
    n_chunks = depth // chunk
    rank = second.shape[2]
    share = rank // n_slab
    partner = (grp, grp + 1 - 2 * lax.rem(grp, 2), lax.rem(grp + 2, 4), 3 - grp)

    def other_slab(distance):
        return lax.rem(slab + distance, n_slab)

    barrier = pltpu.get_barrier_semaphore()
    for relation in (1, 2, 3):
        pl.semaphore_signal(barrier, inc=1, device_id=(slab, partner[relation]), device_id_type=MESH)

    def greet(distance, carry):
        pl.semaphore_signal(barrier, inc=1, device_id=(other_slab(distance), grp), device_id_type=MESH)
        return carry

    lax.fori_loop(1, n_slab, greet, 0)

    cols = pl.ds(pl.multiple_of(grp * LANES, LANES), LANES)
    loads = [
        pltpu.make_async_copy(meta, metas.at[0], load_sem.at[0]),
        pltpu.make_async_copy(omega2, second, load_sem.at[1]),
        pltpu.make_async_copy(omega3.at[:, :, cols], third, load_sem.at[2]),
        pltpu.make_async_copy(blocks, held.at[0], load_sem.at[3]),
    ]
    for load in loads:
        load.start()
    pl.semaphore_wait(barrier, 3 + n_slab - 1)

    def meta_copy(relation):
        return pltpu.make_async_remote_copy(
            src_ref=meta, dst_ref=metas.at[relation],
            send_sem=meta_send.at[relation], recv_sem=meta_recv.at[relation],
            device_id=(slab, partner[relation]), device_id_type=MESH,
        )

    def block_copy(relation, position):
        rows = pl.ds(position * chunk, chunk)
        source = held.at[2, :, rows] if relation == 3 else blocks.at[:, rows]
        target = partner[1] if relation == 3 else partner[relation]
        return pltpu.make_async_remote_copy(
            src_ref=source, dst_ref=held.at[relation, :, rows],
            send_sem=block_send.at[relation, position], recv_sem=block_recv.at[relation, position],
            device_id=(slab, target), device_id_type=MESH,
        )

    for relation in (1, 2, 3):
        meta_copy(relation).start()

    def send_blocks(position, carry):
        block_copy(2, position).start()
        block_copy(1, position).start()
        return carry

    lax.fori_loop(0, n_chunks, send_blocks, 0)

    for relation in (1, 2, 3):
        meta_copy(relation).wait()
    for load in loads:
        load.wait()
    to_scalars = pltpu.make_async_copy(metas, places, load_sem.at[0])
    to_scalars.start()
    to_scalars.wait()

    for relation in range(4):
        for slot in range(n_slots):
            live = places[relation, 2, slot].astype(jnp.float32)
            rows = second[places[relation, 1, slot]].astype(jnp.float32) * live
            place = (relation * n_slots + slot) * edge
            second_cat[:, place:place + edge] = rows.T.astype(jnp.bfloat16)

    def contract_third(relation, position):
        for slot in range(n_slots):
            part = held[relation, slot, pl.ds(position * chunk, chunk)].reshape(chunk * edge, edge)
            product = jnp.dot(part, third[places[relation, 0, slot]], preferred_element_type=jnp.float32)
            product = product.astype(jnp.bfloat16)
            place = (relation * n_slots + slot) * edge
            for row in range(chunk):
                after_cat[place:place + edge, row * LANES:(row + 1) * LANES] = product[row * edge:(row + 1) * edge]

    def fold_copy(distance, position):
        rows = pl.ds(position * chunk, chunk)
        target = other_slab(distance)
        return pltpu.make_async_remote_copy(
            src_ref=folded.at[target, rows], dst_ref=out.at[slab, rows],
            send_sem=fold_send.at[target], recv_sem=fold_recv.at[slab],
            device_id=(target, grp), device_id_type=MESH,
        )

    def step(position, carry):
        block_copy(2, position).wait_recv()
        block_copy(3, position).start()
        contract_third(0, position)
        contract_third(2, position)
        block_copy(1, position).wait_recv()
        contract_third(1, position)
        block_copy(3, position).wait_recv()
        contract_third(3, position)
        summed = jnp.dot(second_cat[...], after_cat[...], preferred_element_type=jnp.float32)
        for target in range(n_slab):
            for row in range(chunk):
                piece = summed[target * share:(target + 1) * share, row * LANES:(row + 1) * LANES]
                folded[target, position * chunk + row] = piece.astype(jnp.bfloat16)

        def send_fold(turn, inner):
            fold_copy(lax.rem(n_slab // 2 - 1 + turn, n_slab - 1) + 1, position).start()
            return inner

        return lax.fori_loop(0, n_slab - 1, send_fold, carry)

    lax.fori_loop(0, n_chunks, step, 0)

    own = pltpu.make_async_copy(folded.at[slab], out.at[slab], own_sem)
    own.start()

    def finish_blocks(position, carry):
        for relation in (1, 2, 3):
            block_copy(relation, position).wait_send()
        return carry

    lax.fori_loop(0, n_chunks, finish_blocks, 0)

    def finish_fold(distance, carry):
        other = other_slab(distance)
        whole = pltpu.make_async_remote_copy(
            src_ref=folded.at[other], dst_ref=out.at[other],
            send_sem=fold_send.at[other], recv_sem=fold_recv.at[other],
            device_id=(other, grp), device_id_type=MESH,
        )
        whole.wait()
        return carry

    lax.fori_loop(1, n_slab, finish_fold, 0)
    own.wait()


def exchange(blocks, meta, omega2, omega3, n_slab, chunk):
    n_slots, depth, edge, _ = blocks.shape
    rank = omega2.shape[2]
    n_chunks = depth // chunk
    live_rows = 4 * n_slots * edge
    anywhere = pl.BlockSpec(memory_space=pl.ANY)
    dma = pltpu.SemaphoreType.DMA
    return pl.pallas_call(
        functools.partial(exchange_kernel, n_slab, chunk),
        out_shape=jax.ShapeDtypeStruct((n_slab, depth, rank // n_slab, LANES), jnp.bfloat16),
        in_specs=[anywhere] * 4,
        out_specs=anywhere,
        scratch_shapes=[
            pltpu.VMEM((4, n_slots, depth, edge, edge), jnp.bfloat16),
            pltpu.VMEM((4, 8, LANES), jnp.int32),
            pltpu.SMEM((4, 8, LANES), jnp.int32),
            pltpu.VMEM(omega2.shape, jnp.bfloat16),
            pltpu.VMEM((*omega3.shape[:2], LANES), jnp.bfloat16),
            pltpu.VMEM((rank, live_rows), jnp.bfloat16),
            pltpu.VMEM((live_rows, chunk * LANES), jnp.bfloat16),
            pltpu.VMEM((n_slab, depth, rank // n_slab, LANES), jnp.bfloat16),
            dma((4,)),
            dma,
            dma((4,)),
            dma((4,)),
            dma((4, n_chunks)),
            dma((4, n_chunks)),
            dma((n_slab,)),
            dma((n_slab,)),
        ],
        compiler_params=pltpu.CompilerParams(
            collective_id=0, has_side_effects=True, vmem_limit_bytes=40 * 2**20
        ),
        cost_estimate=pl.CostEstimate(
            flops=2 * live_rows * depth * LANES * (edge + rank),
            bytes_accessed=24 * 2**20, transcendentals=0,
        ),
        name="exchange",
    )(blocks, meta, omega2, omega3)


def core_kernel(received, omega1, out, wide, by_row, weights):
    n_slab, depth, share, _ = received.shape
    rows, rank = omega1.shape

    @pl.when(pl.program_id(0) == 0)
    def _():
        weights[...] = omega1[...].astype(jnp.float32).T.astype(jnp.bfloat16)

    def spread(slab, carry):
        for row in range(depth):
            wide[pl.ds(slab * depth + row, share, stride=rows), :] = received[slab, row].astype(jnp.float32)
        return carry

    lax.fori_loop(0, n_slab, spread, 0)
    for column in range(share):
        by_row[:, column * LANES:(column + 1) * LANES] = wide[
            column * rows:(column + 1) * rows, :
        ].astype(jnp.bfloat16)
    flat = out.reshape(rank * share, LANES)
    for column in range(0, share, 2):
        product = jnp.dot(
            weights[...], by_row[:, column * LANES:(column + 2) * LANES], preferred_element_type=jnp.float32
        )
        for side in range(2):
            flat[pl.ds(column + side, rank, stride=share), :] = product[:, side * LANES:(side + 1) * LANES]


def core(received, omega1):
    n_slab, depth, share, _ = received.shape
    rows, rank = omega1.shape
    tile = min(16, share)
    return pl.pallas_call(
        core_kernel,
        grid=(share // tile,),
        out_shape=jax.ShapeDtypeStruct((rank, share, LANES), jnp.float32),
        in_specs=[
            pl.BlockSpec((n_slab, depth, tile, LANES), lambda t: (0, 0, t, 0)),
            pl.BlockSpec((rows, rank), lambda t: (0, 0)),
        ],
        out_specs=pl.BlockSpec((rank, tile, LANES), lambda t: (0, t, 0)),
        scratch_shapes=[
            pltpu.VMEM((tile * rows, LANES), jnp.float32),
            pltpu.VMEM((rows, tile * LANES), jnp.bfloat16),
            pltpu.VMEM((rank, rows), jnp.bfloat16),
        ],
        compiler_params=pltpu.CompilerParams(vmem_limit_bytes=40 * 2**20),
        cost_estimate=pl.CostEstimate(
            flops=2 * rank * rows * share * LANES,
            bytes_accessed=rank * share * LANES * 4, transcendentals=0,
        ),
        name="core",
    )(received, omega1)


def local(n_slab, blocks, coords, counts, omega1, omega2, omega3):
    own_blocks = blocks[0]
    n_slots, depth, edge, _ = own_blocks.shape
    corners = coords[0, 0]
    omega2 = omega2.reshape(-1, edge, omega2.shape[1])
    omega3 = omega3.reshape(-1, edge, omega3.shape[1])
    live = (jnp.arange(n_slots) < counts[0, 0]).astype(jnp.int32)
    meta = jnp.stack([corners[:, 1], corners[:, 0], live])
    meta = jnp.pad(meta, ((0, 5), (0, LANES - n_slots)))
    received = exchange(own_blocks, meta, omega2, omega3, n_slab, 2)
    return core(received, omega1)


def solution(mesh):
    in_specs = (
        P("grp", None, "slab", None, None),
        P("grp", "slab", None, None),
        P("grp", "slab"),
        P(),
        P(),
        P(),
    )
    out_specs = P(None, "slab", "grp")
    body = functools.partial(local, mesh.shape["slab"])
    return jax.shard_map(body, mesh=mesh, in_specs=in_specs, out_specs=out_specs, check_vma=False)
```

time: 321 us -> 82.7 us (0.26)
  waiting for transfers between devices: 182 us -> 0 us
  Pallas kernels: 0 us -> 76.2 us
  blocking collectives: 53.6 us -> 0 us
  local copies, waits for them, and re-layouts: 43.6 us -> 5.54 us
  matrix products: 23.3 us -> 0 us
  between operations: 13.4 us -> 0.69 us
    reduce_scatter x1 -> x0, waiting for transfers between devices: 182 us -> none  [local(): lax.psum_scatter(sketch, 'grp', scatter_dimension=0, tiled=True)]
    pallas_call x0 -> x2, Pallas kernels: none -> 76.2 us  [the longest x1 63.9 us: exchange(): pl.pallas_call(functools.partial(exchange_kernel, n_slab, chunk), out_sha...]
    all_to_all x1 -> x0, blocking collectives: 53.6 us -> none  [local(): lax.all_to_all(reduced, 'slab', split_axis=2, concat_axis=1, tiled=True)]
    dot_general x2 -> x0, matrix products: 23.3 us -> none  [the longest x1 15.1 us: contract(): jnp.einsum('ias,ar->sir', after_third, second_rows, preferred_element_typ...]
    while x1 -> x0, local copies, waits for them, and re-layouts: 17.7 us -> none  [local(): sketch = lax.fori_loop(0, live_count, own_step, empty_sketch)]
    transpose x1 -> x0, local copies, waits for them, and re-layouts: 16.5 us -> none  [local(): jnp.einsum('ir,sip->rps', omega1, folded, preferred_element_type=jnp.floa...]
    broadcast_in_dim x1 -> x0, local copies, waits for them, and re-layouts: 8.31 us -> none  [local(): jnp.zeros((omega3.shape[1], slab_depth, sketch_width), jnp.float32)]
    unnamed x4 -> x8, local copies, waits for them, and re-layouts: 0.01 us -> 4.77 us
  transfers between devices with their start and end apart: 1 -> 0, of which waited for: 1 -> 0; matrix products, arithmetic and copies ran while one was open for 0% -> 0% of each run, Pallas kernels for 0% -> 0%
where the time goes in v1:
time: 82.7 us; the launch traced here: 82.5 us
  Pallas kernels  76.2 us (92%)
  local copies, waits for them, and re-layouts  5.54 us (7%)
    pallas_call x1, Pallas kernels, exchange(): pl.pallas_call(functools.partial(exchange_kernel, n_slab, chunk), out_sha...  63.9 us
    pallas_call x1, Pallas kernels, core(): pl.pallas_call(core_kernel, grid=(share // tile,), out_shape=jax.ShapeDty...  12.3 us
    unnamed x8, local copies, waits for them, and re-layouts  4.77 us

profile of v1, /device:TPU:0, one launch (start us, length us, event | category | flops | bytes accessed | tf_op | source)
XLA Modules:
  0.0 82.5 jit_solution(9660833397138717927)
XLA Ops:
  0.7 0.8 slice_bitcast_fusion.1
  1.4 0.0 copy-start.1
  1.5 1.6 %copy-done.1 = bf16[1,4,16,128,128]{4,3,2,1,0:T(8,128)(2,1)S(1)} copy-done((bf16[1,4,16,128,128]{4,3,2,1,0:T(8,128)(2,1)S(1)}, bf16[1,4,16,128,128]{4,3,2,1,0:T(8,128)(2,1)}, u32[]{:S(2)}) %copy-start.1) | copy-done | bytes 2097176
  3.0 0.0 copy-start.2
  3.0 1.6 %copy-done.2 = bf16[2048,512]{1,0:T(8,128)(2,1)S(1)} copy-done((bf16[2048,512]{1,0:T(8,128)(2,1)S(1)}, bf16[2048,512]{1,0:T(8,128)(2,1)}, u32[]{:S(2)}) %copy-start.2) | copy-done | bytes 2097176
  4.6 0.0 copy-start.3
  4.6 1.6 %copy-done.3 = bf16[2048,512]{1,0:T(8,128)(2,1)S(1)} copy-done((bf16[2048,512]{1,0:T(8,128)(2,1)S(1)}, bf16[2048,512]{1,0:T(8,128)(2,1)}, u32[]{:S(2)}) %copy-start.3) | copy-done | bytes 2097176
  6.2 0.0 copy-start
  6.2 63.9 %exchange.1.received = bf16[8,16,64,128]{3,2,1,0:T(8,128)(2,1)S(1)} custom-call(bf16[4,16,128,128]{3,2,1,0:T(8,128)(2,1)S(1)} %bitcast.10, s32[8,128]{1,0:T(8,128)S(1)} %pad.4.meta, bf16[16,128,512]{2,1,0:T(8,128)(2,1)S(1)} %bitcast.11, bf16[16,128,512]{2,1,0:T(8,128)(2,1)S(1)} %bitcast.12), custom_call_target="tpu_custom_call" | custom-call | flops 5368709120 | bytes 25165824 | tf_op jit(solution)/shard_map/exchange/pallas_call | solution.py:164
  70.1 0.0 copy-done
  70.1 12.3 %core.1 = f32[512,64,128]{2,1,0:T(8,128)} custom-call(bf16[8,16,64,128]{3,2,1,0:T(8,128)(2,1)S(1)} %exchange.1.received, bf16[128,512]{1,0:T(8,128)(2,1)S(1)} %copy-done), custom_call_target="tpu_custom_call" | custom-call | flops 1073741824 | bytes 16777216 | tf_op jit(solution)/shard_map/core/pallas_call | solution.py:229
  (3 shorter events, 0.0 us)
Async XLA Ops:
  1.4 1.6 %copy-start.1 = (bf16[1,4,16,128,128]{4,3,2,1,0:T(8,128)(2,1)S(1)}, bf16[1,4,16,128,128]{4,3,2,1,0:T(8,128)(2,1)}, u32[]{:S(2)}) copy-start(bf16[1,4,16,128,128]{4,3,2,1,0:T(8,128)(2,1)} %param.6) | copy-start | bytes 6291460
  3.0 1.6 %copy-start.2 = (bf16[2048,512]{1,0:T(8,128)(2,1)S(1)}, bf16[2048,512]{1,0:T(8,128)(2,1)}, u32[]{:S(2)}) copy-start(bf16[2048,512]{1,0:T(8,128)(2,1)} %param.10) | copy-start | bytes 6291460
  4.6 1.6 %copy-start.3 = (bf16[2048,512]{1,0:T(8,128)(2,1)S(1)}, bf16[2048,512]{1,0:T(8,128)(2,1)}, u32[]{:S(2)}) copy-start(bf16[2048,512]{1,0:T(8,128)(2,1)} %param.11) | copy-start | bytes 6291460
  6.2 63.9 %copy-start = (bf16[128,512]{1,0:T(8,128)(2,1)S(1)}, bf16[128,512]{1,0:T(8,128)(2,1)}, u32[]{:S(2)}) copy-start(bf16[128,512]{1,0:T(8,128)(2,1)} %omega1.1) | copy-start | bytes 393220

commit v2 on v1

--- a/solution.py
+++ b/solution.py
@@ -87,7 +87,7 @@
             live = places[relation, 2, slot].astype(jnp.float32)
             rows = second[places[relation, 1, slot]].astype(jnp.float32) * live
             place = (relation * n_slots + slot) * edge
-            second_cat[:, place:place + edge] = rows.T.astype(jnp.bfloat16)
+            second_cat[:, place:place + edge] = rows.astype(jnp.bfloat16).T
 
     def contract_third(relation, position):
         for slot in range(n_slots):
@@ -185,7 +185,7 @@
             dma((n_slab,)),
         ],
         compiler_params=pltpu.CompilerParams(
-            collective_id=0, has_side_effects=True, vmem_limit_bytes=40 * 2**20
+            collective_id=0, has_side_effects=True, vmem_limit_bytes=62 * 2**20
         ),
         cost_estimate=pl.CostEstimate(
             flops=2 * live_rows * depth * LANES * (edge + rank),
@@ -195,24 +195,29 @@
     )(blocks, meta, omega2, omega3)
 
 
-def core_kernel(received, omega1, out, wide, by_row, weights):
+def core_kernel(received, omega1, out, by_row, weights, swap):
     n_slab, depth, share, _ = received.shape
     rows, rank = omega1.shape
+    size = depth * share
 
     @pl.when(pl.program_id(0) == 0)
     def _():
         weights[...] = omega1[...].astype(jnp.float32).T.astype(jnp.bfloat16)
-
-    def spread(slab, carry):
-        for row in range(depth):
-            wide[pl.ds(slab * depth + row, share, stride=rows), :] = received[slab, row].astype(jnp.float32)
-        return carry
-
-    lax.fori_loop(0, n_slab, spread, 0)
-    for column in range(share):
-        by_row[:, column * LANES:(column + 1) * LANES] = wide[
-            column * rows:(column + 1) * rows, :
-        ].astype(jnp.bfloat16)
+        to_place = lax.broadcasted_iota(jnp.int32, (size, size), 0)
+        from_place = lax.broadcasted_iota(jnp.int32, (size, size), 1)
+        wanted = lax.rem(to_place, depth) * share + lax.div(to_place, depth)
+        swap[...] = (from_place == wanted).astype(jnp.float32).astype(jnp.bfloat16)
+
+    for slab in range(n_slab):
+        natural = received[slab]
+        if share % 16:
+            natural = natural.astype(jnp.float32)
+        natural = natural.reshape(size, LANES).astype(jnp.bfloat16)
+        moved = jnp.dot(swap[...], natural, preferred_element_type=jnp.float32).astype(jnp.bfloat16)
+        for column in range(share):
+            by_row[slab * depth:(slab + 1) * depth, column * LANES:(column + 1) * LANES] = moved[
+                column * depth:(column + 1) * depth
+            ]
     flat = out.reshape(rank * share, LANES)
     for column in range(0, share, 2):
         product = jnp.dot(
@@ -236,9 +241,9 @@
         ],
         out_specs=pl.BlockSpec((rank, tile, LANES), lambda t: (0, t, 0)),
         scratch_shapes=[
-            pltpu.VMEM((tile * rows, LANES), jnp.float32),
             pltpu.VMEM((rows, tile * LANES), jnp.bfloat16),
             pltpu.VMEM((rank, rows), jnp.bfloat16),
+            pltpu.VMEM((depth * tile, depth * tile), jnp.bfloat16),
         ],
         compiler_params=pltpu.CompilerParams(vmem_limit_bytes=40 * 2**20),
         cost_estimate=pl.CostEstimate(
@@ -258,7 +263,7 @@
     live = (jnp.arange(n_slots) < counts[0, 0]).astype(jnp.int32)
     meta = jnp.stack([corners[:, 1], corners[:, 0], live])
     meta = jnp.pad(meta, ((0, 5), (0, LANES - n_slots)))
-    received = exchange(own_blocks, meta, omega2, omega3, n_slab, 2)
+    received = exchange(own_blocks, meta, omega2, omega3, n_slab, 1)
     return core(received, omega1)
 
 

time: 82.7 us -> 75.2 us (0.909)
  Pallas kernels: 76.2 us -> 71.4 us
  local copies, waits for them, and re-layouts: 5.54 us -> 2.95 us
    unnamed x8 -> x4, local copies, waits for them, and re-layouts: 4.77 us -> 1.59 us
    pallas_call x1, Pallas kernels: 12.3 us -> 9.59 us  [core(): pl.pallas_call(core_kernel, grid=(share // tile,), out_shape=jax.ShapeDty...]
    pallas_call x1, Pallas kernels: 63.9 us -> 61.8 us  [exchange(): pl.pallas_call(functools.partial(exchange_kernel, n_slab, chunk), out_sha...]
where the time goes in v2:
time: 75.2 us; the launch traced here: 75.1 us
  Pallas kernels  71.4 us (95%)
  local copies, waits for them, and re-layouts  2.95 us (4%)
    pallas_call x1, Pallas kernels, exchange(): pl.pallas_call(functools.partial(exchange_kernel, n_slab, chunk), out_sha...  61.8 us
    pallas_call x1, Pallas kernels, core(): pl.pallas_call(core_kernel, grid=(share // tile,), out_shape=jax.ShapeDty...  9.59 us
    unnamed x4, local copies, waits for them, and re-layouts  1.59 us

profile of v2, /device:TPU:0, one launch (start us, length us, event | category | flops | bytes accessed | tf_op | source)
XLA Modules:
  0.0 75.1 jit_solution(1132465357085748789)
XLA Ops:
  0.7 0.8 %slice_bitcast_fusion.1 = (s32[1,4]{1,0:T(1,128)S(1)}, s32[1,4]{1,0:T(1,128)S(1)}) fusion(s32[4,2]{0,1:T(2,128)} %bitcast.10), kind=kLoop, calls=%fused_computation.3 | loop fusion | bytes 64 | tf_op jit(solution)/shard_map/stack;squeeze | solution.py:264
  1.4 0.6 pad.4.meta
  2.0 0.0 copy-start.1
  2.0 61.8 %exchange.1.received = bf16[8,16,64,128]{3,2,1,0:T(8,128)(2,1)} custom-call(bf16[4,16,128,128]{3,2,1,0:T(8,128)(2,1)} %bitcast.11, s32[8,128]{1,0:T(8,128)} %pad.4.meta, bf16[16,128,512]{2,1,0:T(8,128)(2,1)} %bitcast.12, bf16[16,128,512]{2,1,0:T(8,128)(2,1)} %bitcast.13), custom_call_target="tpu_custom_call" | custom-call | flops 5368709120 | bytes 25165824 | tf_op jit(solution)/shard_map/exchange/pallas_call | solution.py:164
  63.9 0.0 copy-done.1
  63.9 0.0 copy-start
  63.9 1.6 %copy-done = bf16[8,16,64,128]{3,2,1,0:T(8,128)(2,1)S(1)} copy-done((bf16[8,16,64,128]{3,2,1,0:T(8,128)(2,1)S(1)}, bf16[8,16,64,128]{3,2,1,0:T(8,128)(2,1)}, u32[]{:S(2)}) %copy-start) | copy-done | bytes 2097176
  65.5 9.6 %core.1 = f32[512,64,128]{2,1,0:T(8,128)} custom-call(bf16[8,16,64,128]{3,2,1,0:T(8,128)(2,1)S(1)} %copy-done, bf16[128,512]{1,0:T(8,128)(2,1)S(1)} %copy-done.1), custom_call_target="tpu_custom_call" | custom-call | flops 1073741824 | bytes 16777216 | tf_op jit(solution)/shard_map/core/pallas_call | solution.py:234
  (2 shorter events, 0.0 us)
Async XLA Ops:
  2.0 61.8 %copy-start.1 = (bf16[128,512]{1,0:T(8,128)(2,1)S(1)}, bf16[128,512]{1,0:T(8,128)(2,1)}, u32[]{:S(2)}) copy-start(bf16[128,512]{1,0:T(8,128)(2,1)} %omega1.1) | copy-start | bytes 393220
  63.9 1.6 %copy-start = (bf16[8,16,64,128]{3,2,1,0:T(8,128)(2,1)S(1)}, bf16[8,16,64,128]{3,2,1,0:T(8,128)(2,1)}, u32[]{:S(2)}) copy-start(bf16[8,16,64,128]{3,2,1,0:T(8,128)(2,1)} %exchange.1.received) | copy-start | bytes 6291460

commit v3 on v2

--- a/solution.py
+++ b/solution.py
@@ -74,6 +74,8 @@
 
     lax.fori_loop(0, n_chunks, send_blocks, 0)
 
+    block_copy(2, 0).wait_recv()
+    block_copy(3, 0).start()
     for relation in (1, 2, 3):
         meta_copy(relation).wait()
     for load in loads:
@@ -85,14 +87,14 @@
     for relation in range(4):
         for slot in range(n_slots):
             live = places[relation, 2, slot].astype(jnp.float32)
-            rows = second[places[relation, 1, slot]].astype(jnp.float32) * live
+            rows = second[places[relation, 0, slot]].astype(jnp.float32) * live
             place = (relation * n_slots + slot) * edge
             second_cat[:, place:place + edge] = rows.astype(jnp.bfloat16).T
 
     def contract_third(relation, position):
         for slot in range(n_slots):
             part = held[relation, slot, pl.ds(position * chunk, chunk)].reshape(chunk * edge, edge)
-            product = jnp.dot(part, third[places[relation, 0, slot]], preferred_element_type=jnp.float32)
+            product = jnp.dot(part, third[places[relation, 1, slot]], preferred_element_type=jnp.float32)
             product = product.astype(jnp.bfloat16)
             place = (relation * n_slots + slot) * edge
             for row in range(chunk):
@@ -108,8 +110,11 @@
         )
 
     def step(position, carry):
-        block_copy(2, position).wait_recv()
-        block_copy(3, position).start()
+        @pl.when(position > 0)
+        def _():
+            block_copy(2, position).wait_recv()
+            block_copy(3, position).start()
+
         contract_third(0, position)
         contract_third(2, position)
         block_copy(1, position).wait_recv()
@@ -195,12 +200,18 @@
     )(blocks, meta, omega2, omega3)
 
 
-def core_kernel(received, omega1, out, by_row, weights, swap):
+def core_kernel(received, omega1, out, by_row, weights, swap, staged, sems):
     n_slab, depth, share, _ = received.shape
     rows, rank = omega1.shape
     size = depth * share
-
-    @pl.when(pl.program_id(0) == 0)
+    step, steps = pl.program_id(0), pl.num_programs(0)
+    part = staged.shape[2]
+
+    def store(turn, half):
+        columns = pl.ds(pl.multiple_of(turn * share + half * part, part), part)
+        return pltpu.make_async_copy(staged.at[half], out.at[:, columns, :], sems.at[half])
+
+    @pl.when(step == 0)
     def _():
         weights[...] = omega1[...].astype(jnp.float32).T.astype(jnp.bfloat16)
         to_place = lax.broadcasted_iota(jnp.int32, (size, size), 0)
@@ -218,19 +229,32 @@
             by_row[slab * depth:(slab + 1) * depth, column * LANES:(column + 1) * LANES] = moved[
                 column * depth:(column + 1) * depth
             ]
-    flat = out.reshape(rank * share, LANES)
-    for column in range(0, share, 2):
-        product = jnp.dot(
-            weights[...], by_row[:, column * LANES:(column + 2) * LANES], preferred_element_type=jnp.float32
-        )
-        for side in range(2):
-            flat[pl.ds(column + side, rank, stride=share), :] = product[:, side * LANES:(side + 1) * LANES]
+    flat = staged.reshape(share * rank, LANES)
+    for half in range(share // part):
+        @pl.when(step > 0)
+        def _():
+            store(step - 1, half).wait()
+
+        for column in range(0, part, 2):
+            place = (half * part + column) * LANES
+            product = jnp.dot(
+                weights[...], by_row[:, place:place + 2 * LANES], preferred_element_type=jnp.float32
+            )
+            for side in range(2):
+                spots = pl.ds(half * rank * part + column + side, rank, stride=part)
+                flat[spots, :] = product[:, side * LANES:(side + 1) * LANES]
+        store(step, half).start()
+
+    @pl.when(step == steps - 1)
+    def _():
+        for half in range(share // part):
+            store(step, half).wait()
 
 
 def core(received, omega1):
     n_slab, depth, share, _ = received.shape
     rows, rank = omega1.shape
-    tile = min(16, share)
+    tile, part = min(16, share), min(8, share)
     return pl.pallas_call(
         core_kernel,
         grid=(share // tile,),
@@ -239,13 +263,15 @@
             pl.BlockSpec((n_slab, depth, tile, LANES), lambda t: (0, 0, t, 0)),
             pl.BlockSpec((rows, rank), lambda t: (0, 0)),
         ],
-        out_specs=pl.BlockSpec((rank, tile, LANES), lambda t: (0, t, 0)),
+        out_specs=pl.BlockSpec(memory_space=pl.ANY),
         scratch_shapes=[
             pltpu.VMEM((rows, tile * LANES), jnp.bfloat16),
             pltpu.VMEM((rank, rows), jnp.bfloat16),
             pltpu.VMEM((depth * tile, depth * tile), jnp.bfloat16),
+            pltpu.VMEM((tile // part, rank, part, LANES), jnp.float32),
+            pltpu.SemaphoreType.DMA((tile // part,)),
         ],
-        compiler_params=pltpu.CompilerParams(vmem_limit_bytes=40 * 2**20),
+        compiler_params=pltpu.CompilerParams(vmem_limit_bytes=62 * 2**20),
         cost_estimate=pl.CostEstimate(
             flops=2 * rank * rows * share * LANES,
             bytes_accessed=rank * share * LANES * 4, transcendentals=0,
@@ -257,12 +283,12 @@
 def local(n_slab, blocks, coords, counts, omega1, omega2, omega3):
     own_blocks = blocks[0]
     n_slots, depth, edge, _ = own_blocks.shape
-    corners = coords[0, 0]
+    row = lax.broadcasted_iota(jnp.int32, (8, LANES), 0)
+    lane = lax.broadcasted_iota(jnp.int32, (8, LANES), 1)
+    corners = jnp.pad(coords[0, 0].T, ((0, 6), (0, LANES - n_slots)))
+    meta = jnp.where(row == 2, (lane < counts[0, 0]).astype(jnp.int32), corners)
     omega2 = omega2.reshape(-1, edge, omega2.shape[1])
     omega3 = omega3.reshape(-1, edge, omega3.shape[1])
-    live = (jnp.arange(n_slots) < counts[0, 0]).astype(jnp.int32)
-    meta = jnp.stack([corners[:, 1], corners[:, 0], live])
-    meta = jnp.pad(meta, ((0, 5), (0, LANES - n_slots)))
     received = exchange(own_blocks, meta, omega2, omega3, n_slab, 1)
     return core(received, omega1)
 

time: 75.2 us -> 73.9 us (0.983)
  local copies, waits for them, and re-layouts: 2.95 us -> 0 us
  other arithmetic: 0.02 us -> 1.35 us
    unnamed x4 -> x0, local copies, waits for them, and re-layouts: 1.59 us -> none
    select_n x0 -> x1, other arithmetic: none -> 1.34 us  [local(): meta = jnp.where(row == 2, (lane < counts[0, 0]).astype(jnp.int32), corners)]
    another operation x1 -> x0, local copies, waits for them, and re-layouts: 0.76 us -> none  [local(): meta = jnp.stack([corners[:, 1], corners[:, 0], live])]
where the time goes in v3:
time: 73.9 us; the launch traced here: 73.7 us
  Pallas kernels  71.7 us (97%)
  other arithmetic  1.35 us (2%)
    pallas_call x1, Pallas kernels, exchange(): pl.pallas_call(functools.partial(exchange_kernel, n_slab, chunk), out_sha...  62.2 us
    pallas_call x1, Pallas kernels, core(): pl.pallas_call(core_kernel, grid=(share // tile,), out_shape=jax.ShapeDty...  9.54 us

profile of v3, /device:TPU:0, one launch (start us, length us, event | category | flops | bytes accessed | tf_op | source)
XLA Modules:
  0.0 73.7 jit_solution(4867876267071829583)
XLA Ops:
  0.7 1.3 %pad_select_fusion.meta = s32[8,128]{1,0:T(8,128)} fusion(s32[2,4]{1,0:T(2,128)} %bitcast.8, s32[128]{0:T(128)S(1)} %compare_convert_fusion, pred[8]{0:T(512)(128)(4,1)S(1)} %iota_compare_fusion), kind=kLoop, calls=%fused_computation | loop fusion | flops 1024 | bytes 4648 | tf_op jit(solution)/shard_map/jit(_where)/select_n | solution.py:289
  2.0 62.2 %exchange.1.received = bf16[8,16,64,128]{3,2,1,0:T(8,128)(2,1)} custom-call(bf16[4,16,128,128]{3,2,1,0:T(8,128)(2,1)} %bitcast.9, s32[8,128]{1,0:T(8,128)} %pad_select_fusion.meta, bf16[16,128,512]{2,1,0:T(8,128)(2,1)} %bitcast.10, bf16[16,128,512]{2,1,0:T(8,128)(2,1)} %bitcast.11), custom_call_target="tpu_custom_call" | custom-call | flops 5368709120 | bytes 25165824 | tf_op jit(solution)/shard_map/exchange/pallas_call | solution.py:169
  64.2 9.5 %core.1 = f32[512,64,128]{2,1,0:T(8,128)} custom-call(bf16[8,16,64,128]{3,2,1,0:T(8,128)(2,1)} %exchange.1.received, bf16[128,512]{1,0:T(8,128)(2,1)} %omega1.1), custom_call_target="tpu_custom_call" | custom-call | flops 1073741824 | bytes 16777216 | tf_op jit(solution)/shard_map/core/pallas_call | solution.py:258
  (2 shorter events, 0.0 us)

commit v4 on v3

--- a/solution.py
+++ b/solution.py
@@ -69,10 +69,14 @@
 
     def send_blocks(position, carry):
         block_copy(2, position).start()
+        return carry
+
+    def send_pair(position, carry):
         block_copy(1, position).start()
         return carry
 
     lax.fori_loop(0, n_chunks, send_blocks, 0)
+    lax.fori_loop(0, n_chunks, send_pair, 0)
 
     block_copy(2, 0).wait_recv()
     block_copy(3, 0).start()

time: 73.9 us -> 73.9 us (level)
  no operation moved by 1% of the time
where the time goes in v4:
time: 73.9 us; the launch traced here: 73.7 us
  Pallas kernels  71.7 us (97%)
  other arithmetic  1.35 us (2%)
    pallas_call x1, Pallas kernels, exchange(): pl.pallas_call(functools.partial(exchange_kernel, n_slab, chunk), out_sha...  62.2 us
    pallas_call x1, Pallas kernels, core(): pl.pallas_call(core_kernel, grid=(share // tile,), out_shape=jax.ShapeDty...  9.54 us

profile of v4, /device:TPU:0, one launch (start us, length us, event | category | flops | bytes accessed | tf_op | source)
XLA Modules:
  0.0 73.7 jit_solution(3996564072059787017)
XLA Ops:
  0.7 1.3 %pad_select_fusion.meta = s32[8,128]{1,0:T(8,128)} fusion(s32[2,4]{1,0:T(2,128)} %bitcast.8, s32[128]{0:T(128)S(1)} %compare_convert_fusion, pred[8]{0:T(512)(128)(4,1)S(1)} %iota_compare_fusion), kind=kLoop, calls=%fused_computation | loop fusion | flops 1024 | bytes 4648 | tf_op jit(solution)/shard_map/jit(_where)/select_n | solution.py:293
  2.0 62.2 %exchange.1.received = bf16[8,16,64,128]{3,2,1,0:T(8,128)(2,1)} custom-call(bf16[4,16,128,128]{3,2,1,0:T(8,128)(2,1)} %bitcast.9, s32[8,128]{1,0:T(8,128)} %pad_select_fusion.meta, bf16[16,128,512]{2,1,0:T(8,128)(2,1)} %bitcast.10, bf16[16,128,512]{2,1,0:T(8,128)(2,1)} %bitcast.11), custom_call_target="tpu_custom_call" | custom-call | flops 5368709120 | bytes 25165824 | tf_op jit(solution)/shard_map/exchange/pallas_call | solution.py:173
  64.2 9.5 %core.1 = f32[512,64,128]{2,1,0:T(8,128)} custom-call(bf16[8,16,64,128]{3,2,1,0:T(8,128)(2,1)} %exchange.1.received, bf16[128,512]{1,0:T(8,128)(2,1)} %omega1.1), custom_call_target="tpu_custom_call" | custom-call | flops 1073741824 | bytes 16777216 | tf_op jit(solution)/shard_map/core/pallas_call | solution.py:262
  (2 shorter events, 0.0 us)
